TPU v7x, 32 devices: a whole 2x2x4 slice. The times are simulated.
32 devices in a mesh: dp: 8 (over z, x), tensor: 4 (over y, core).
Axes of the slice: x: 2, y: 2, z: 4, core: 2. Of those that a mesh axis runs over, the one named last changes fastest.
Arguments:
- layer_input: float32 [8, 1024, 768], P('dp', 'tensor'), may hold values from -40 to 40
- out_cotangent: float32 [8, 1024, 768], P('dp', 'tensor'), may hold values from -6 to 6
- mix_gain: bfloat16 [768], P('dp'), may hold values from 0.099609375 to 1.8984375
- mix_shift: bfloat16 [768], P('dp'), may hold values from -4 to 4
- query_weight: bfloat16 [768, 768], P('dp', 'tensor'), may hold values from -2 to 2
- query_bias: bfloat16 [64, 12], P('dp', 'tensor'), may hold values from -3 to 3
- key_weight: bfloat16 [768, 768], P('dp', 'tensor'), may hold values from -2 to 2
- value_weight: bfloat16 [768, 768], P('dp', 'tensor'), may hold values from -0.21875 to 0.21875
- value_bias: bfloat16 [64, 12], P('dp', 'tensor'), may hold values from -0.59765625 to 0.59765625
- output_weight: bfloat16 [768, 768], P('dp', 'tensor'), may hold values from -1.75 to 1.75
- output_bias: bfloat16 [768], P('dp'), may hold values from -4 to 4
- feed_gain: bfloat16 [768], P('dp'), may hold values from 0.099609375 to 1.8984375
- feed_shift: bfloat16 [768], P('dp'), may hold values from -4 to 4
- inner_weight: bfloat16 [768, 3072], P('dp', 'tensor'), may hold values from -0.21875 to 0.21875
- inner_bias: bfloat16 [64, 48], P('dp', 'tensor'), may hold values from -3 to 3
- outer_weight: bfloat16 [768, 3072], P('dp', 'tensor'), may hold values from -0.3125 to 0.3125
- outer_bias: bfloat16 [768], P('dp'), may hold values from -4 to 4
Outputs:
- layer_output: float32 [8, 1024, 768], P('dp', 'tensor')
- input_grad: float32 [8, 1024, 768], P('dp', 'tensor')
- mix_gain_grad: float32 [768], P(('dp', 'tensor'))
- mix_shift_grad: float32 [768], P(('dp', 'tensor'))
- query_weight_grad: float32 [768, 768], P('dp', 'tensor')
- query_bias_grad: float32 [64, 12], P('dp', 'tensor')
- key_weight_grad: float32 [768, 768], P('dp', 'tensor')
- value_weight_grad: float32 [768, 768], P('dp', 'tensor')
- value_bias_grad: float32 [64, 12], P('dp', 'tensor')
- output_weight_grad: float32 [768, 768], P('dp', 'tensor')
- output_bias_grad: float32 [768], P(('dp', 'tensor'))
- feed_gain_grad: float32 [768], P(('dp', 'tensor'))
- feed_shift_grad: float32 [768], P(('dp', 'tensor'))
- inner_weight_grad: float32 [768, 3072], P('dp', 'tensor')
- inner_bias_grad: float32 [64, 48], P('dp', 'tensor')
- outer_weight_grad: float32 [768, 3072], P('dp', 'tensor')
- outer_bias_grad: float32 [768], P(('dp', 'tensor'))
All inputs are finite; a program needn't handle non-finite values.
Results may differ from a plain program's by a relative error of at most 0.02.
Values may be sent and summed in bfloat16 or wider, within the bound.
A program may use at most 128 MiB of HBM per device.

v0:
```python
import math
import jax
import jax.numpy as jnp
from jax import lax
from jax.sharding import PartitionSpec as P

HD = 64
EPS = 1e-05
ROOT_HALF = 0.7071067811865476
DENSITY_NORM = 0.3989422804014327


def layer_norm(block, gain, shift):
    row_mean = jnp.mean(block, axis=-1, keepdims=True)
    centred = block - row_mean
    rstd = lax.rsqrt(jnp.mean(centred * centred, axis=-1, keepdims=True) + EPS)
    normed = centred * rstd
    lowered = (normed * gain.astype(jnp.float32) + shift.astype(jnp.float32)).astype(jnp.bfloat16)
    return (normed, rstd, lowered)


def norm_backward(gradient, normed, rstd, gain):
    scaled = gradient * gain.astype(jnp.float32)
    first = jnp.mean(scaled, axis=-1, keepdims=True)
    second = jnp.mean(scaled * normed, axis=-1, keepdims=True)
    return (scaled - first - normed * second) * rstd


def gelu_value(preact):
    return 0.5 * preact * (1.0 + lax.erf(preact * ROOT_HALF))


def gelu_slope(preact):
    return 0.5 * (1.0 + lax.erf(preact * ROOT_HALF)) + preact * DENSITY_NORM * jnp.exp(
        -0.5 * preact * preact
    )


def matmul(left, right):
    return jnp.dot(left, right, preferred_element_type=jnp.float32)


def token_product(left, right):
    return lax.dot_general(
        left, right, (((0,), (0,)), ((), ())), preferred_element_type=jnp.float32
    )


def split_heads(block):
    return block.reshape(block.shape[0], block.shape[1] // HD, HD)


def attend(operands):
    queries, key_rows, values = operands
    score_scale = 1.0 / math.sqrt(HD)
    scores = (
        jnp.einsum(
            "qhd,khd->hqk",
            split_heads(queries),
            split_heads(key_rows),
            preferred_element_type=jnp.float32,
        )
        * score_scale
    )
    row_max = jnp.max(scores, axis=-1, keepdims=True)
    log_total = row_max + jnp.log(jnp.sum(jnp.exp(scores - row_max), axis=-1, keepdims=True))
    prob_low = jnp.exp(scores - log_total).astype(jnp.bfloat16)
    context = jnp.einsum(
        "hqk,khd->qhd", prob_low, split_heads(values), preferred_element_type=jnp.float32
    )
    return (context.reshape(queries.shape).astype(jnp.bfloat16), log_total)


def attend_back(operands):
    queries, key_rows, values, context_grad, log_total = operands
    score_scale = 1.0 / math.sqrt(HD)
    query_heads = split_heads(queries)
    key_heads = split_heads(key_rows)
    grad_heads = split_heads(context_grad)
    scores = (
        jnp.einsum("qhd,khd->hqk", query_heads, key_heads, preferred_element_type=jnp.float32)
        * score_scale
    )
    prob_full = jnp.exp(scores - log_total)
    prob_low = prob_full.astype(jnp.bfloat16)
    value_grad = jnp.einsum(
        "hqk,qhd->khd", prob_low, grad_heads, preferred_element_type=jnp.float32
    )
    prob_grad = jnp.einsum(
        "qhd,khd->hqk", grad_heads, split_heads(values), preferred_element_type=jnp.float32
    )
    row_dot = jnp.sum(prob_full * prob_grad, axis=-1, keepdims=True)
    score_grad = (prob_full * (prob_grad - row_dot) * score_scale).astype(jnp.bfloat16)
    query_grad = jnp.einsum(
        "hqk,khd->qhd", score_grad, key_heads, preferred_element_type=jnp.float32
    )
    key_low = jnp.einsum(
        "hqk,qhd->khd", score_grad, query_heads, preferred_element_type=jnp.float32
    ).astype(jnp.bfloat16)
    return (
        query_grad.reshape(queries.shape),
        key_low.reshape(queries.shape),
        value_grad.reshape(queries.shape),
    )


def on_device(
    layer_input,
    out_cotangent,
    mix_gain,
    mix_shift,
    query_weight,
    query_bias,
    key_weight,
    value_weight,
    value_bias,
    output_weight,
    output_bias,
    feed_gain,
    feed_shift,
    inner_weight,
    inner_bias,
    outer_weight,
    outer_bias,
):
    (
        gain_first,
        shift_first,
        query_full,
        bias_query,
        key_full,
        value_full,
        bias_value,
        output_full,
        bias_output,
        gain_second,
        shift_second,
        inner_full,
        bias_inner,
        outer_full,
        bias_outer,
    ) = (
        lax.all_gather(mix_gain, "dp", axis=0, tiled=True),
        lax.all_gather(mix_shift, "dp", axis=0, tiled=True),
        lax.all_gather(query_weight, "dp", axis=0, tiled=True),
        lax.all_gather(query_bias, "dp", axis=0, tiled=True),
        lax.all_gather(key_weight, "dp", axis=0, tiled=True),
        lax.all_gather(value_weight, "dp", axis=0, tiled=True),
        lax.all_gather(value_bias, "dp", axis=0, tiled=True),
        lax.all_gather(output_weight, "dp", axis=0, tiled=True),
        lax.all_gather(output_bias, "dp", axis=0, tiled=True),
        lax.all_gather(feed_gain, "dp", axis=0, tiled=True),
        lax.all_gather(feed_shift, "dp", axis=0, tiled=True),
        lax.all_gather(inner_weight, "dp", axis=0, tiled=True),
        lax.all_gather(inner_bias, "dp", axis=0, tiled=True),
        lax.all_gather(outer_weight, "dp", axis=0, tiled=True),
        lax.all_gather(outer_bias, "dp", axis=0, tiled=True),
    )
    clip_count = layer_input.shape[0]
    feature_count = layer_input.shape[2]
    normed_one, rstd_one, lowered_one = layer_norm(layer_input, gain_first, shift_first)
    gathered_one = lax.all_gather(lowered_one, "tensor", axis=1, tiled=True)
    frames = gathered_one.shape[1]
    flat_one = gathered_one.reshape(clip_count * frames, feature_count)
    vector_query = bias_query.astype(jnp.float32).T.reshape(-1)
    vector_value = bias_value.astype(jnp.float32).T.reshape(-1)
    vector_inner = bias_inner.astype(jnp.float32).T.reshape(-1)
    width = query_full.shape[1]
    queries = (matmul(flat_one, query_full) + vector_query).astype(jnp.bfloat16)
    key_rows = matmul(flat_one, key_full).astype(jnp.bfloat16)
    values = (matmul(flat_one, value_full) + vector_value).astype(jnp.bfloat16)
    clip_queries = queries.reshape(clip_count, frames, width)
    clip_keys = key_rows.reshape(clip_count, frames, width)
    clip_values = values.reshape(clip_count, frames, width)
    context, log_total = lax.map(attend, (clip_queries, clip_keys, clip_values))
    flat_context = context.reshape(clip_count * frames, width)
    attn_partial = matmul(flat_context, output_full.T).reshape(clip_count, frames, feature_count)
    attn_share = lax.psum_scatter(
        attn_partial.astype(jnp.bfloat16), "tensor", scatter_dimension=1, tiled=True
    ).astype(jnp.float32)
    mixed = layer_input + attn_share + bias_output.astype(jnp.float32)
    normed_two, rstd_two, lowered_two = layer_norm(mixed, gain_second, shift_second)
    gathered_two = lax.all_gather(lowered_two, "tensor", axis=1, tiled=True)
    flat_two = gathered_two.reshape(clip_count * frames, feature_count)
    preact = matmul(flat_two, inner_full) + vector_inner
    hidden = gelu_value(preact).astype(jnp.bfloat16)
    feed_partial = matmul(hidden, outer_full.T).reshape(clip_count, frames, feature_count)
    feed_share = lax.psum_scatter(
        feed_partial.astype(jnp.bfloat16), "tensor", scatter_dimension=1, tiled=True
    ).astype(jnp.float32)
    layer_output = mixed + feed_share + bias_outer.astype(jnp.float32)
    cot_low = out_cotangent.astype(jnp.bfloat16)
    cot_all = lax.all_gather(cot_low, "tensor", axis=1, tiled=True).reshape(
        clip_count * frames, feature_count
    )
    preact_grad = matmul(cot_all, outer_full) * gelu_slope(preact)
    preact_low = preact_grad.astype(jnp.bfloat16)
    outer_grad = token_product(cot_all, hidden)
    inner_grad = token_product(flat_two, preact_low)
    inner_bias_part = jnp.sum(preact_grad, axis=0).reshape(-1, HD).T
    norm_two_part = matmul(preact_low, inner_full.T).reshape(clip_count, frames, feature_count)
    norm_two_grad = lax.psum_scatter(
        norm_two_part.astype(jnp.bfloat16), "tensor", scatter_dimension=1, tiled=True
    ).astype(jnp.float32)
    feed_gain_part = jnp.sum(norm_two_grad * normed_two, axis=(0, 1))
    feed_shift_part = jnp.sum(norm_two_grad, axis=(0, 1))
    mixed_grad = out_cotangent + norm_backward(norm_two_grad, normed_two, rstd_two, gain_second)
    outer_bias_part = jnp.sum(out_cotangent, axis=(0, 1))
    output_bias_part = jnp.sum(mixed_grad, axis=(0, 1))
    mixed_low = mixed_grad.astype(jnp.bfloat16)
    mixed_all = lax.all_gather(mixed_low, "tensor", axis=1, tiled=True).reshape(
        clip_count * frames, feature_count
    )
    output_grad = token_product(mixed_all, flat_context)
    context_grad = (
        matmul(mixed_all, output_full).astype(jnp.bfloat16).reshape(clip_count, frames, width)
    )
    query_grad, key_low, value_grad = lax.map(
        attend_back, (clip_queries, clip_keys, clip_values, context_grad, log_total)
    )
    query_grad = query_grad.reshape(clip_count * frames, width)
    key_low = key_low.reshape(clip_count * frames, width)
    value_grad = value_grad.reshape(clip_count * frames, width)
    query_low = query_grad.astype(jnp.bfloat16)
    value_low = value_grad.astype(jnp.bfloat16)
    query_grad_part = token_product(flat_one, query_low)
    key_grad_part = token_product(flat_one, key_low)
    value_grad_part = token_product(flat_one, value_low)
    query_bias_part = jnp.sum(query_grad, axis=0).reshape(-1, HD).T
    value_bias_part = jnp.sum(value_grad, axis=0).reshape(-1, HD).T
    norm_one_part = (
        matmul(query_low, query_full.T)
        + matmul(key_low, key_full.T)
        + matmul(value_low, value_full.T)
    )
    norm_one_grad = lax.psum_scatter(
        norm_one_part.reshape(clip_count, frames, feature_count).astype(jnp.bfloat16),
        "tensor",
        scatter_dimension=1,
        tiled=True,
    ).astype(jnp.float32)
    mix_gain_part = jnp.sum(norm_one_grad * normed_one, axis=(0, 1))
    mix_shift_part = jnp.sum(norm_one_grad, axis=(0, 1))
    input_grad = mixed_grad + norm_backward(norm_one_grad, normed_one, rstd_one, gain_first)
    (
        query_weight_grad,
        query_bias_grad,
        key_weight_grad,
        value_weight_grad,
        value_bias_grad,
        output_weight_grad,
        inner_weight_grad,
        inner_bias_grad,
        outer_weight_grad,
    ) = (
        lax.psum_scatter(query_grad_part, "dp", scatter_dimension=0, tiled=True),
        lax.psum_scatter(query_bias_part, "dp", scatter_dimension=0, tiled=True),
        lax.psum_scatter(key_grad_part, "dp", scatter_dimension=0, tiled=True),
        lax.psum_scatter(value_grad_part, "dp", scatter_dimension=0, tiled=True),
        lax.psum_scatter(value_bias_part, "dp", scatter_dimension=0, tiled=True),
        lax.psum_scatter(output_grad, "dp", scatter_dimension=0, tiled=True),
        lax.psum_scatter(inner_grad, "dp", scatter_dimension=0, tiled=True),
        lax.psum_scatter(inner_bias_part, "dp", scatter_dimension=0, tiled=True),
        lax.psum_scatter(outer_grad, "dp", scatter_dimension=0, tiled=True),
    )
    (
        mix_gain_grad,
        mix_shift_grad,
        output_bias_grad,
        feed_gain_grad,
        feed_shift_grad,
        outer_bias_grad,
    ) = (
        lax.psum_scatter(mix_gain_part, ("dp", "tensor"), scatter_dimension=0, tiled=True),
        lax.psum_scatter(mix_shift_part, ("dp", "tensor"), scatter_dimension=0, tiled=True),
        lax.psum_scatter(output_bias_part, ("dp", "tensor"), scatter_dimension=0, tiled=True),
        lax.psum_scatter(feed_gain_part, ("dp", "tensor"), scatter_dimension=0, tiled=True),
        lax.psum_scatter(feed_shift_part, ("dp", "tensor"), scatter_dimension=0, tiled=True),
        lax.psum_scatter(outer_bias_part, ("dp", "tensor"), scatter_dimension=0, tiled=True),
    )
    return (
        layer_output,
        input_grad,
        mix_gain_grad,
        mix_shift_grad,
        query_weight_grad,
        query_bias_grad,
        key_weight_grad,
        value_weight_grad,
        value_bias_grad,
        output_weight_grad,
        output_bias_grad,
        feed_gain_grad,
        feed_shift_grad,
        inner_weight_grad,
        inner_bias_grad,
        outer_weight_grad,
        outer_bias_grad,
    )


def solution(mesh):
    placed = (
        P("dp", "tensor", None),
        P("dp", "tensor", None),
        P("dp"),
        P("dp"),
        P("dp", "tensor"),
        P("dp", "tensor"),
        P("dp", "tensor"),
        P("dp", "tensor"),
        P("dp", "tensor"),
        P("dp", "tensor"),
        P("dp"),
        P("dp"),
        P("dp"),
        P("dp", "tensor"),
        P("dp", "tensor"),
        P("dp", "tensor"),
        P("dp"),
    )
    return jax.shard_map(
        on_device,
        mesh=mesh,
        in_specs=placed,
        out_specs=(
            P("dp", "tensor", None),
            P("dp", "tensor", None),
            P(("dp", "tensor")),
            P(("dp", "tensor")),
            P("dp", "tensor"),
            P("dp", "tensor"),
            P("dp", "tensor"),
            P("dp", "tensor"),
            P("dp", "tensor"),
            P("dp", "tensor"),
            P(("dp", "tensor")),
            P(("dp", "tensor")),
            P(("dp", "tensor")),
            P("dp", "tensor"),
            P("dp", "tensor"),
            P("dp", "tensor"),
            P(("dp", "tensor")),
        ),
        check_vma=False,
    )
```

profile of v0, /device:TPU:0, one launch (start us, length us, event | category | flops | bytes accessed | tf_op | source)
XLA Modules:
  0.0 955.9 jit_solution(9160846206304437627)
XLA Ops:
  8.1 1.3 reduce_sum.173
  9.4 1.4 multiply_reduce_fusion.3
  10.8 1.3 fusion.107
  12.8 0.8 dynamic-update-slice.3
  13.7 0.8 dynamic-update-slice.4
  17.8 38.8 %all-reduce.17 = (bf16[768]{0:T(1024)(128)(2,1)S(1)}, bf16[768]{0:T(1024)(128)(2,1)S(1)}, bf16[768]{0:T(1024)(128)(2,1)S(1)}, bf16[768]{0:T(1024)(128)(2,1)S(1)}...) all-reduce(bf16[768]{0:T(1024)(128)(2,1)S(1)} %dynamic-update-slice., ...), channel_id=1, replica_groups=mesh['dp'=8,'tensor'=4] {'dp'}, use_global_device_ids=true, to_apply=%add.1 | all-reduce | flops 4608 | bytes 18432
  56.6 2.1 add_convert_fusion.2
  58.8 16.6 %all-gather.1 = bf16[8,8,3]{1,2,0:T(4,128)(2,1)S(1)} all-gather(bf16[1,8,3]{1,2,0:T(4,128)(2,1)S(1)} %bitcast.145), channel_id=1, replica_groups=mesh['dp'=8,'tensor'=4] {'dp'}, dimensions={0}, use_global_device_ids=true | all-gather | bytes 432 | tf_op jit(solution)/shard_map/all_gather | solution.py:146
  75.6 17.9 %all-gather = bf16[8,8,3]{1,2,0:T(4,128)(2,1)S(1)} all-gather(bf16[1,8,3]{1,2,0:T(4,128)(2,1)S(1)} %bitcast.146), channel_id=1, replica_groups=mesh['dp'=8,'tensor'=4] {'dp'}, dimensions={0}, use_global_device_ids=true | all-gather | bytes 432 | tf_op jit(solution)/shard_map/all_gather | solution.py:149
  93.7 31.1 %all_gather.62 = bf16[768,192]{1,0:T(8,128)(2,1)S(1)} all-gather(bf16[96,192]{1,0:T(8,128)(2,1)S(1)} %copy-done.22), channel_id=1, replica_groups=mesh['dp'=8,'tensor'=4] {'dp'}, dimensions={0}, use_global_device_ids=true | all-gather | bytes 331776 | tf_op jit(solution)/shard_map/all_gather | solution.py:145
  124.8 31.1 %all_gather.64 = bf16[768,192]{1,0:T(8,128)(2,1)S(1)} all-gather(bf16[96,192]{1,0:T(8,128)(2,1)S(1)} %copy-done.23), channel_id=1, replica_groups=mesh['dp'=8,'tensor'=4] {'dp'}, dimensions={0}, use_global_device_ids=true | all-gather | bytes 331776 | tf_op jit(solution)/shard_map/all_gather | solution.py:147
  155.9 31.1 %all_gather.60 = bf16[768,192]{1,0:T(8,128)(2,1)S(1)} all-gather(bf16[96,192]{1,0:T(8,128)(2,1)S(1)} %copy-done.24), channel_id=1, replica_groups=mesh['dp'=8,'tensor'=4] {'dp'}, dimensions={0}, use_global_device_ids=true | all-gather | bytes 331776 | tf_op jit(solution)/shard_map/all_gather | solution.py:148
  187.0 31.0 %all_gather.65 = bf16[768,192]{1,0:T(8,128)(2,1)S(1)} all-gather(bf16[96,192]{1,0:T(8,128)(2,1)S(1)} %copy-done.25), channel_id=1, replica_groups=mesh['dp'=8,'tensor'=4] {'dp'}, dimensions={0}, use_global_device_ids=true | all-gather | bytes 331776 | tf_op jit(solution)/shard_map/all_gather | solution.py:150
  217.9 2.2 fusion.58
  220.2 2.2 fusion.64
  222.4 1.9 multiply_reduce_fusion.1
  224.3 2.1 exponential_reduce_fusion
  227.6 1.5 copy-done
  229.0 2.2 convolution_convert_fusion.3
  232.0 1.8 fusion.45
  236.3 23.1 %reduce-scatter.16.cloned.1.call-done = bf16[1,256,768]{2,1,0:T(8,128)(2,1)} async-done(((bf16[1,1024,768]{2,1,0:T(8,128)(2,1)}), bf16[1,256,768]{2,1,0:T(8,128)(2,1)}) %reduce-scatter.16.cloned.1.call-update) | async-done | bytes 393232 | tf_op jit(solution)/shard_map/reduce_scatter | solution.py:178
  259.4 1.2 fusion.103
  261.7 1.6 add_convert_fusion.1
  264.0 2.9 fusion.106
  267.0 26.2 %all_gather.71 = bf16[64,12]{1,0:T(8,128)(2,1)S(1)} all-gather(bf16[8,12]{1,0:T(8,128)(2,1)} %param.31), channel_id=1, replica_groups=mesh['dp'=8,'tensor'=4] {'dp'}, dimensions={0}, use_global_device_ids=true | all-gather | bytes 1728 | tf_op jit(solution)/shard_map/all_gather | solution.py:155
  293.8 1.4 copy.60
  295.2 1.4 reshape.253
  296.6 5.5 multiply_convert_fusion.1
  302.1 37.3 %all-gather.15.cloned.1.call-done = bf16[768,768]{1,0:T(8,128)(2,1)} async-done(((bf16[96,768]{1,0:T(8,128)(2,1)}), bf16[768,768]{1,0:T(8,128)(2,1)}) %all-gather.15.cloned.1.call-update) | async-done | bytes 1179664 | tf_op jit(solution)/shard_map/all_gather | solution.py:156
  339.4 20.3 %all-gather.17.cloned.1.call-done = bf16[1,1024,768]{2,1,0:T(8,128)(2,1)} async-done(((bf16[1,256,768]{2,1,0:T(8,128)(2,1)}), bf16[1,1024,768]{2,1,0:T(8,128)(2,1)}) %all-gather.17.cloned.1.call-update) | async-done | bytes 1572880 | tf_op jit(solution)/shard_map/all_gather | solution.py:193
  359.7 5.5 fusion.110
  365.2 1.2 copy-done.34
  366.4 2.6 fusion.47
  369.0 4.4 fusion.46
  373.4 1.3 convert_element_type.153
  374.7 22.6 %reduce-scatter.20.cloned.1.call-done = bf16[1,256,768]{2,1,0:T(8,128)(2,1)} async-done(((bf16[1,1024,768]{2,1,0:T(8,128)(2,1)}), bf16[1,256,768]{2,1,0:T(8,128)(2,1)}) %reduce-scatter.20.cloned.1.call-update) | async-done | bytes 393232 | tf_op jit(solution)/shard_map/reduce_scatter | solution.py:202
  397.3 2.0 fusion.89
  399.9 28.0 %reduce-scatter.18.cloned.1.call-done = bf16[1,256,768]{2,1,0:T(8,128)(2,1)} async-done(((bf16[1,1024,768]{2,1,0:T(8,128)(2,1)}), bf16[1,256,768]{2,1,0:T(8,128)(2,1)}) %reduce-scatter.18.cloned.1.call-update) | async-done | bytes 393232 | tf_op jit(solution)/shard_map/reduce_scatter | solution.py:188
  427.9 3.3 fusion.101
  431.2 0.9 copy-done.3
  433.0 19.6 %all-gather.19.cloned.1.call-done = bf16[1,1024,768]{2,1,0:T(8,128)(2,1)} async-done(((bf16[1,256,768]{2,1,0:T(8,128)(2,1)}), bf16[1,1024,768]{2,1,0:T(8,128)(2,1)}) %all-gather.19.cloned.1.call-update) | async-done | bytes 1572880 | tf_op jit(solution)/shard_map/all_gather | solution.py:211
  452.5 2.1 fusion.61
  454.6 7.5 fusion.104
  462.2 6.3 fusion.111
  468.5 19.8 %fusion.70 = bf16[3,64,1024]{2,1,0:T(8,128)(2,1)} fusion(bf16[1024,3,64]{0,2,1:T(8,128)(2,1)S(1)} %bitcast.135, f32[3,1024,1024]{1,2,0:T(8,128)} %fusion.111, f32[3,1024,1024]{1,2,0:T(8,128)} %copy-done, f32[3,1024]{1,0:T(4,128)S(1)} %log_add_fusion), kind=kOutput, calls=%fused_computation.61 | convolution fusion | flops 431165440 | bytes 25964544 | tf_op jit(solution)/shard_map/while/body/eval_jaxpr/hqk,qhd->khd/dot_general | solution.py:97
  488.3 20.0 %fusion.105 = (f32[3,64]{1,0:T(4,128)}, bf16[1024,3,64]{0,2,1:T(8,128)(2,1)}) fusion(bf16[1024,3,64]{0,2,1:T(8,128)(2,1)S(1)} %bitcast.133, f32[3,1024,1024]{1,2,0:T(8,128)} %fusion.111, f32[3,1024,1024]{1,2,0:T(8,128)} %copy-done, f32[3,1024]{1,0:T(4,128)S(1)} %log_add_fusion), kind=kOutput, calls=%fused_computation.118 | convolution fusion | flops 431361856 | bytes 25965312 | tf_op jit(solution)/shard_map/while/body/eval_jaxpr/hqk,khd->qhd/dot_general | solution.py:94
  508.3 1.7 fusion.113
  510.7 1.9 fusion.48
  512.6 4.7 fusion.29
  517.4 4.8 convolution_bitcast_fusion
  522.3 3.1 copy.76
  525.7 2.9 fusion.23
  528.7 1.6 fusion.33
  530.3 1.6 fusion.35
  533.5 1.5 fusion.37
  535.0 37.5 %all-reduce.16 = (f32[64,3]{0,1:T(4,128)S(1)}, f32[64,3]{0,1:T(4,128)S(1)}, f32[64,12]{0,1:T(8,128)S(1)}) all-reduce(f32[64,3]{0,1:T(4,128)} %bitcast.144, f32[64,3]{0,1:T(4,128)} %bitcast.143, f32[64,12]{0,1:T(8,128)S(1)} %bitcast.140), channel_id=9, replica_groups=mesh['dp'=8,'tensor'=4] {'dp'}, use_global_device_ids=true, to_apply=%region_21.22.clone | all-reduce | flops 1152 | bytes 9216
  574.6 1.4 fusion.90
  576.0 37.7 %all-reduce.15 = (f32[768]{0:T(1024)S(1)}, f32[768]{0:T(1024)S(1)}, f32[768]{0:T(1024)S(1)}, f32[768]{0:T(1024)S(1)}, f32[768]{0:T(1024)S(1)}, /*index=5*/f32[768]{0:T(1024)S(1)}) all-reduce(f32[768]{0:T(1024)S(1)} %get-tuple-element.132, f32[768]{0:T(1024)S(1)} %get-tuple-element.137, ...), channel_id=6, replica_groups=mesh['dp'=8,'tensor'=4] {'dp','tensor'}, use_global_device_ids=true, to_apply=%region_16.17.clone | all-reduce | flops 4608 | bytes 36864
  617.2 2.2 fusion.83
  619.4 66.7 %reduce-scatter.34.cloned.1.call-done = f32[96,768]{1,0:T(8,128)} async-done(((f32[768,768]{1,0:T(8,128)}), f32[96,768]{1,0:T(8,128)}) %reduce-scatter.34.cloned.1.call-update) | async-done | bytes 294928
  686.1 65.4 %reduce-scatter.30.cloned.1.call-done = f32[96,192]{1,0:T(8,128)} async-done(((f32[768,192]{1,0:T(8,128)}), f32[96,192]{1,0:T(8,128)}) %reduce-scatter.30.cloned.1.call-update) | async-done | bytes 73744 | tf_op jit(solution)/shard_map/reduce_scatter | solution.py:261
  751.5 65.8 %reduce-scatter.28.cloned.1.call-done = f32[96,192]{1,0:T(8,128)} async-done(((f32[768,192]{1,0:T(8,128)}), f32[96,192]{1,0:T(8,128)}) %reduce-scatter.28.cloned.1.call-update) | async-done | bytes 73744 | tf_op jit(solution)/shard_map/reduce_scatter | solution.py:259
  817.3 65.4 %reduce-scatter.26.cloned.1.call-done = f32[96,192]{1,0:T(8,128)} async-done(((f32[768,192]{1,0:T(8,128)}), f32[96,192]{1,0:T(8,128)}) %reduce-scatter.26.cloned.1.call-update) | async-done | bytes 73744 | tf_op jit(solution)/shard_map/reduce_scatter | solution.py:258
  882.7 65.8 %reduce-scatter.24.cloned.1.call-done = f32[96,192]{1,0:T(8,128)} async-done(((f32[768,192]{1,0:T(8,128)}), f32[96,192]{1,0:T(8,128)}) %reduce-scatter.24.cloned.1.call-update) | async-done | bytes 73744 | tf_op jit(solution)/shard_map/reduce_scatter | solution.py:256
  (149 shorter events, 19.7 us)
Async XLA Ops:
  8.0 50.8 %copy-start.31 = (bf16[8,3]{0,1:T(4,128)(2,1)S(1)}, bf16[8,3]{0,1:T(4,128)(2,1)}, u32[]{:S(2)}) copy-start(bf16[8,3]{0,1:T(4,128)(2,1)} %param.22) | copy-start | bytes 148
  8.0 67.6 %copy-start.32 = (bf16[8,3]{0,1:T(4,128)(2,1)S(1)}, bf16[8,3]{0,1:T(4,128)(2,1)}, u32[]{:S(2)}) copy-start(bf16[8,3]{0,1:T(4,128)(2,1)} %param.25) | copy-start | bytes 148
  8.0 85.7 %copy-start.22 = (bf16[96,192]{1,0:T(8,128)(2,1)S(1)}, bf16[96,192]{1,0:T(8,128)(2,1)}, u32[]{:S(2)}) copy-start(bf16[96,192]{1,0:T(8,128)(2,1)} %param.21) | copy-start | bytes 110596
  8.1 116.8 %copy-start.23 = (bf16[96,192]{1,0:T(8,128)(2,1)S(1)}, bf16[96,192]{1,0:T(8,128)(2,1)}, u32[]{:S(2)}) copy-start(bf16[96,192]{1,0:T(8,128)(2,1)} %param.23) | copy-start | bytes 110596
  8.1 147.8 %copy-start.24 = (bf16[96,192]{1,0:T(8,128)(2,1)S(1)}, bf16[96,192]{1,0:T(8,128)(2,1)}, u32[]{:S(2)}) copy-start(bf16[96,192]{1,0:T(8,128)(2,1)} %param.24) | copy-start | bytes 110596
  8.1 178.9 %copy-start.25 = (bf16[96,192]{1,0:T(8,128)(2,1)S(1)}, bf16[96,192]{1,0:T(8,128)(2,1)}, u32[]{:S(2)}) copy-start(bf16[96,192]{1,0:T(8,128)(2,1)} %param.26) | copy-start | bytes 110596
  8.1 209.9 %all-gather.9.cloned.1.call-start = ((), (), s32[]{:S(2)}) async-start(), calls=%async_computation.10 | async-start | bytes 1966080 | tf_op jit(solution)/shard_map/all_gather | solution.py:162
  9.4 49.4 %copy-start.26 = (f32[256]{0:T(256)}, f32[256]{0:T(256)S(1)}, u32[]{:S(2)}) copy-start(f32[256]{0:T(256)S(1)} %broadcast_multiply_fusion.5) | copy-start | bytes 3076
  10.8 48.0 %copy-start.29 = (f32[256]{0:T(256)}, f32[256]{0:T(256)S(1)}, u32[]{:S(2)}) copy-start(f32[256]{0:T(256)S(1)} %add_rsqrt_fusion.1) | copy-start | bytes 3076
  56.6 68.2 %copy-start.20 = (f32[768]{0:T(1024)}, f32[768]{0:T(1024)S(1)}, u32[]{:S(2)}) copy-start(f32[768]{0:T(1024)S(1)} %convert_element_type.132) | copy-start | bytes 9220
  58.8 200.6 %reduce-scatter.16.cloned.1.call-start = ((), (), s32[]{:S(2)}) async-start(), calls=%async_computation.11 | async-start | bytes 1966080 | tf_op jit(solution)/shard_map/reduce_scatter | solution.py:178
  124.8 99.5 %copy-start.12 = (bf16[768,192]{1,0:T(8,128)(2,1)}, bf16[768,192]{1,0:T(8,128)(2,1)S(1)}, u32[]{:S(2)}) copy-start(bf16[768,192]{1,0:T(8,128)(2,1)S(1)} %all_gather.62) | copy-start | bytes 884740
  155.9 68.4 %copy-start.10 = (bf16[768,192]{1,0:T(8,128)(2,1)}, bf16[768,192]{1,0:T(8,128)(2,1)S(1)}, u32[]{:S(2)}) copy-start(bf16[768,192]{1,0:T(8,128)(2,1)S(1)} %all_gather.64) | copy-start | bytes 884740
  187.0 39.4 %copy-start.7 = (bf16[768,192]{1,0:T(8,128)(2,1)}, bf16[768,192]{1,0:T(8,128)(2,1)S(1)}, u32[]{:S(2)}) copy-start(bf16[768,192]{1,0:T(8,128)(2,1)S(1)} %all_gather.60) | copy-start | bytes 884740
  217.9 13.4 %copy-start.9 = (bf16[768,192]{1,0:T(8,128)(2,1)}, bf16[768,192]{1,0:T(8,128)(2,1)S(1)}, u32[]{:S(2)}) copy-start(bf16[768,192]{1,0:T(8,128)(2,1)S(1)} %all_gather.65) | copy-start | bytes 884740
  220.2 4.1 copy-start.14
  222.4 1.9 copy-start.16
  224.3 4.7 copy-start
  224.3 2.6 copy-start.1
  231.3 0.7 copy-start.5
  231.3 28.1 %copy-start.2 = (f32[1,256,768]{2,1,0:T(8,128)S(1)}, f32[1,256,768]{2,1,0:T(8,128)}, u32[]{:S(2)}) copy-start(f32[1,256,768]{2,1,0:T(8,128)} %param.17) | copy-start | bytes 2359300
  233.9 62.7 %all-gather.13.cloned.1.call-start = ((), (), s32[]{:S(2)}) async-start(), calls=%async_computation.13 | async-start | bytes 1327104 | tf_op jit(solution)/shard_map/all_gather | solution.py:154
  234.5 62.1 %all-gather.11.cloned.1.call-start = ((), (), s32[]{:S(2)}) async-start(), calls=%async_computation.12 | async-start | bytes 1966080 | tf_op jit(solution)/shard_map/all_gather | solution.py:183
  260.6 0.6 copy-start.28
  261.2 0.6 copy-start.30
  263.4 76.0 %all-gather.15.cloned.1.call-start = ((), (), s32[]{:S(2)}) async-start(), calls=%async_computation.14 | async-start | bytes 1327104 | tf_op jit(solution)/shard_map/all_gather | solution.py:156
  264.0 95.7 %all-gather.17.cloned.1.call-start = ((), (), s32[]{:S(2)}) async-start(), calls=%async_computation.16 | async-start | bytes 1966080 | tf_op jit(solution)/shard_map/all_gather | solution.py:193
  266.9 130.4 %reduce-scatter.20.cloned.1.call-start = ((), (), s32[]{:S(2)}) async-start(), calls=%async_computation.17 | async-start | bytes 1966080 | tf_op jit(solution)/shard_map/reduce_scatter | solution.py:202
  359.7 6.7 copy-start.33
  365.2 1.2 copy-start.34
  369.0 59.0 %reduce-scatter.18.cloned.1.call-start = ((), (), s32[]{:S(2)}) async-start(), calls=%async_computation.15 | async-start | bytes 1966080 | tf_op jit(solution)/shard_map/reduce_scatter | solution.py:188
  373.4 79.1 %all-gather.19.cloned.1.call-start = ((), (), s32[]{:S(2)}) async-start(), calls=%async_computation.18 | async-start | bytes 1966080 | tf_op jit(solution)/shard_map/all_gather | solution.py:211
  431.2 0.9 copy-start.3
  432.9 141.7 %reduce-scatter.22.cloned.1.call-start = ((), (), s32[]{:S(2)}) async-start(), calls=%async_computation.19 | async-start | bytes 1966080 | tf_op jit(solution)/shard_map/reduce_scatter | solution.py:236
  462.2 6.3 copy-start.17
  468.5 19.8 %copy-start.15 = (bf16[1024,192]{0,1:T(8,128)(2,1)S(1)}, bf16[1024,192]{0,1:T(8,128)(2,1)}, u32[]{:S(2)}) copy-start(bf16[1024,192]{0,1:T(8,128)(2,1)} %copy-done.14) | copy-start | bytes 1179652
  488.3 20.0 %copy-start.11 = (bf16[768,192]{1,0:T(8,128)(2,1)S(1)}, bf16[768,192]{1,0:T(8,128)(2,1)}, u32[]{:S(2)}) copy-start(bf16[768,192]{1,0:T(8,128)(2,1)} %copy-done.10) | copy-start | bytes 884740
  508.3 1.7 copy-start.13
  508.3 1.7 copy-start.18
  508.3 2.4 copy-start.8
  512.6 106.8 %reduce-scatter.32.cloned.1.call-start = ((), (), s32[]{:S(2)}) async-start(), calls=%async_computation.24 | async-start | bytes 2654208 | tf_op jit(solution)/shard_map/reduce_scatter | solution.py:262
  517.4 168.7 %reduce-scatter.34.cloned.1.call-start = ((), (), s32[]{:S(2)}) async-start(), calls=%async_computation.25 | async-start | bytes 2654208
  522.3 3.4 copy-start.6
  525.4 226.1 %reduce-scatter.30.cloned.1.call-start = ((), (), s32[]{:S(2)}) async-start(), calls=%async_computation.23 | async-start | bytes 884736 | tf_op jit(solution)/shard_map/reduce_scatter | solution.py:261
  528.6 1.7 copy-start.19
  528.6 288.7 %reduce-scatter.28.cloned.1.call-start = ((), (), s32[]{:S(2)}) async-start(), calls=%async_computation.22 | async-start | bytes 884736 | tf_op jit(solution)/shard_map/reduce_scatter | solution.py:259
  530.2 44.3 %copy-start.21 = (f32[768]{0:T(1024)S(1)}, f32[768]{0:T(1024)}, u32[]{:S(2)}) copy-start(f32[768]{0:T(1024)} %copy-done.20) | copy-start | bytes 9220
  530.2 44.3 %copy-start.27 = (f32[256]{0:T(256)S(1)}, f32[256]{0:T(256)}, u32[]{:S(2)}) copy-start(f32[256]{0:T(256)} %copy-done.26) | copy-start | bytes 3076
  530.3 352.4 %reduce-scatter.26.cloned.1.call-start = ((), (), s32[]{:S(2)}) async-start(), calls=%async_computation.21 | async-start | bytes 884736 | tf_op jit(solution)/shard_map/reduce_scatter | solution.py:258
  531.9 85.3 %copy-start.4 = (f32[1,256,768]{2,1,0:T(8,128)S(1)}, f32[1,256,768]{2,1,0:T(8,128)}, u32[]{:S(2)}) copy-start(f32[1,256,768]{2,1,0:T(8,128)} %copy-done.3) | copy-start | bytes 2359300
  531.9 416.6 %reduce-scatter.24.cloned.1.call-start = ((), (), s32[]{:S(2)}) async-start(), calls=%async_computation.20 | async-start | bytes 884736 | tf_op jit(solution)/shard_map/reduce_scatter | solution.py:256
Sparse Core Ops, SparseCore 0:
  58.9 16.9 all-gather.8
  234.0 25.3 reduce-scatter.15
  369.1 28.1 reduce-scatter.19
  399.7 28.1 reduce-scatter.17
Sparse Core Ops, SparseCore 1:
  236.8 38.6 all-gather.12
  277.6 18.0 all-gather.10
  297.9 41.5 all-gather.14
  341.7 18.0 all-gather.16
  433.0 19.5 all-gather.18
  512.7 28.1 reduce-scatter.21
  544.7 69.3 reduce-scatter.31
  618.0 68.0 reduce-scatter.33
  689.9 61.6 reduce-scatter.29
  755.8 61.5 reduce-scatter.27
  821.1 61.5 reduce-scatter.25
  886.9 61.5 reduce-scatter.23
where the time goes:
time: 965 us; the launch traced here: 956 us
  waiting for transfers between devices  481 us (50%)
  blocking collectives  299 us (31%)
  matrix products  106 us (11%)
  other arithmetic  26.7 us (3%)
  local copies, waits for them, and re-layouts  24.5 us (3%)
  between operations  17.4 us (2%)
    unnamed x3, blocking collectives  114 us
    unnamed x17, waiting for transfers between devices  67.5 us
    reduce_scatter x1, waiting for transfers between devices, on_device(): lax.psum_scatter(query_grad_part, 'dp', scatter_dimension=0, tiled=True)  65.8 us
    reduce_scatter x1, waiting for transfers between devices, on_device(): lax.psum_scatter(value_grad_part, 'dp', scatter_dimension=0, tiled=True)  65.8 us
    reduce_scatter x1, waiting for transfers between devices, on_device(): lax.psum_scatter(output_grad, 'dp', scatter_dimension=0, tiled=True)  65.4 us
    reduce_scatter x1, waiting for transfers between devices, on_device(): lax.psum_scatter(key_grad_part, 'dp', scatter_dimension=0, tiled=True)  65.4 us
    all_gather x1, waiting for transfers between devices, on_device(): lax.all_gather(outer_weight, 'dp', axis=0, tiled=True)  37.3 us
    dot_general x12, matrix products, matmul(): return jnp.dot(left, right, preferred_element_type=jnp.float32)  31.2 us
  transfers between devices with their start and end apart: 16, of which 11 were waited for; matrix products, arithmetic and copies ran while one was open for 6% of the time, Pallas kernels for 0%

commit v1 on v0

--- a/solution.py
+++ b/solution.py
@@ -8,6 +8,26 @@
 EPS = 1e-05
 ROOT_HALF = 0.7071067811865476
 DENSITY_NORM = 0.3989422804014327
+
+
+def apply_skins(message, axis_k):
+    out_arr = list(message.shape[1:])
+    out_arr[axis_k] *= message.shape[0]
+    return jnp.moveaxis(message, 0, axis_k).reshape(out_arr)
+
+
+def fit_sums_all_over_axis(s0, mesh_ax):
+    n_all = lax.axis_size(mesh_ax)
+    a_now = s0[None]
+    for k0 in range(n_all.bit_length() - 1):
+        even = 1 << k0
+        w1 = lax.ppermute(
+            a_now, axis_name=mesh_ax, perm=list(map(lambda s: (s, s ^ even), range(n_all)))
+        )
+        local_part = jnp.stack([a_now, w1], axis=0)
+        main = lax.axis_index(mesh_ax) >> k0 & 1
+        a_now = jnp.where(main == 0, local_part, local_part[::-1]).reshape(-1, *s0.shape)
+    return a_now
 
 
 def layer_norm(block, gain, shift):
@@ -123,6 +143,10 @@
     outer_weight,
     outer_bias,
 ):
+
+    def mark_regions(row_data, inputs, ndim_at):
+        return apply_skins(fit_sums_all_over_axis(row_data, inputs), ndim_at)
+
     (
         gain_first,
         shift_first,
@@ -153,7 +177,7 @@
         lax.all_gather(feed_shift, "dp", axis=0, tiled=True),
         lax.all_gather(inner_weight, "dp", axis=0, tiled=True),
         lax.all_gather(inner_bias, "dp", axis=0, tiled=True),
-        lax.all_gather(outer_weight, "dp", axis=0, tiled=True),
+        mark_regions(outer_weight, "dp", 0),
         lax.all_gather(outer_bias, "dp", axis=0, tiled=True),
     )
     clip_count = layer_input.shape[0]

time: 965 us -> 947 us (0.981)
  waiting for transfers between devices: 481 us -> 432 us
  blocking collectives: 299 us -> 317 us
    all_gather x1 -> x0, waiting for transfers between devices: 37.3 us -> none  [on_device(): lax.all_gather(outer_weight, 'dp', axis=0, tiled=True)]
    all_gather x1, waiting for transfers between devices: 20.3 us -> 0.01 us  [on_device(): lax.all_gather(cot_low, 'tensor', axis=1, tiled=True)]
    all_gather x1, blocking collectives: 26.2 us -> 43.3 us  [on_device(): lax.all_gather(inner_bias, 'dp', axis=0, tiled=True)]
    ppermute x0 -> x3, waiting for transfers between devices: none -> 9.85 us  [fit_sums_all_over_axis(): lax.ppermute(a_now, axis_name=mesh_ax, perm=list(map(lambda s: (s, s ^ ev...]
    unnamed x17 -> x16, waiting for transfers between devices: 67.5 us -> 67.9 us
  transfers between devices with their start and end apart: 16 -> 18, of which waited for: 11 -> 11; matrix products, arithmetic and copies ran while one was open for 6% -> 7% of each run, Pallas kernels for 0% -> 0%
where the time goes in v1:
time: 947 us; the launch traced here: 937 us
  waiting for transfers between devices  432 us (46%)
  blocking collectives  317 us (33%)
  matrix products  106 us (11%)
  other arithmetic  33.3 us (4%)
  local copies, waits for them, and re-layouts  24.6 us (3%)
  between operations  17.6 us (2%)
    unnamed x3, blocking collectives  115 us
    unnamed x16, waiting for transfers between devices  67.9 us
    reduce_scatter x1, waiting for transfers between devices, on_device(): lax.psum_scatter(value_grad_part, 'dp', scatter_dimension=0, tiled=True)  65.7 us
    reduce_scatter x1, waiting for transfers between devices, on_device(): lax.psum_scatter(query_grad_part, 'dp', scatter_dimension=0, tiled=True)  65.7 us
    reduce_scatter x1, waiting for transfers between devices, on_device(): lax.psum_scatter(key_grad_part, 'dp', scatter_dimension=0, tiled=True)  65.5 us
    reduce_scatter x1, waiting for transfers between devices, on_device(): lax.psum_scatter(output_grad, 'dp', scatter_dimension=0, tiled=True)  65.4 us
    all_gather x1, blocking collectives, on_device(): lax.all_gather(inner_bias, 'dp', axis=0, tiled=True)  43.3 us
    dot_general x12, matrix products, matmul(): return jnp.dot(left, right, preferred_element_type=jnp.float32)  31.2 us
  transfers between devices with their start and end apart: 18, of which 11 were waited for; matrix products, arithmetic and copies ran while one was open for 7% of the time, Pallas kernels for 0%

profile of v1, /device:TPU:0, one launch (start us, length us, event | category | flops | bytes accessed | tf_op | source)
XLA Modules:
  0.0 937.0 jit_solution(1337025346662386990)
XLA Ops:
  8.1 1.3 reduce_sum.173
  9.4 1.4 multiply_reduce_fusion.3
  10.8 1.3 fusion.109
  17.8 38.8 %all-reduce.17 = (bf16[768]{0:T(1024)(128)(2,1)S(1)}, bf16[768]{0:T(1024)(128)(2,1)S(1)}, bf16[768]{0:T(1024)(128)(2,1)S(1)}, bf16[768]{0:T(1024)(128)(2,1)S(1)}...) all-reduce(bf16[768]{0:T(1024)(128)(2,1)S(1)} %dynamic-update-slice., ...), channel_id=1, replica_groups=mesh['dp'=8,'tensor'=4] {'dp'}, use_global_device_ids=true, to_apply=%add.1 | all-reduce | flops 4608 | bytes 18432
  56.6 2.1 add_convert_fusion.2
  58.8 16.6 %all-gather.1 = bf16[8,8,3]{1,2,0:T(4,128)(2,1)S(1)} all-gather(bf16[1,8,3]{1,2,0:T(4,128)(2,1)S(1)} %bitcast.163), channel_id=1, replica_groups=mesh['dp'=8,'tensor'=4] {'dp'}, dimensions={0}, use_global_device_ids=true | all-gather | bytes 432 | tf_op jit(solution)/shard_map/all_gather | solution.py:170
  75.6 17.9 %all-gather = bf16[8,8,3]{1,2,0:T(4,128)(2,1)S(1)} all-gather(bf16[1,8,3]{1,2,0:T(4,128)(2,1)S(1)} %bitcast.164), channel_id=1, replica_groups=mesh['dp'=8,'tensor'=4] {'dp'}, dimensions={0}, use_global_device_ids=true | all-gather | bytes 432 | tf_op jit(solution)/shard_map/all_gather | solution.py:173
  93.7 31.1 %all_gather.59 = bf16[768,192]{1,0:T(8,128)(2,1)S(1)} all-gather(bf16[96,192]{1,0:T(8,128)(2,1)S(1)} %copy-done.22), channel_id=1, replica_groups=mesh['dp'=8,'tensor'=4] {'dp'}, dimensions={0}, use_global_device_ids=true | all-gather | bytes 331776 | tf_op jit(solution)/shard_map/all_gather | solution.py:169
  124.8 31.1 %all_gather.61 = bf16[768,192]{1,0:T(8,128)(2,1)S(1)} all-gather(bf16[96,192]{1,0:T(8,128)(2,1)S(1)} %copy-done.23), channel_id=1, replica_groups=mesh['dp'=8,'tensor'=4] {'dp'}, dimensions={0}, use_global_device_ids=true | all-gather | bytes 331776 | tf_op jit(solution)/shard_map/all_gather | solution.py:171
  155.9 31.1 %all_gather.57 = bf16[768,192]{1,0:T(8,128)(2,1)S(1)} all-gather(bf16[96,192]{1,0:T(8,128)(2,1)S(1)} %copy-done.24), channel_id=1, replica_groups=mesh['dp'=8,'tensor'=4] {'dp'}, dimensions={0}, use_global_device_ids=true | all-gather | bytes 331776 | tf_op jit(solution)/shard_map/all_gather | solution.py:172
  187.0 31.0 %all_gather.62 = bf16[768,192]{1,0:T(8,128)(2,1)S(1)} all-gather(bf16[96,192]{1,0:T(8,128)(2,1)S(1)} %copy-done.25), channel_id=1, replica_groups=mesh['dp'=8,'tensor'=4] {'dp'}, dimensions={0}, use_global_device_ids=true | all-gather | bytes 331776 | tf_op jit(solution)/shard_map/all_gather | solution.py:174
  217.9 2.2 fusion.58
  220.2 2.2 fusion.64
  222.4 1.9 multiply_reduce_fusion.1
  224.3 2.1 exponential_reduce_fusion
  227.6 1.5 copy-done
  229.0 2.2 convolution_convert_fusion.3
  232.0 1.8 fusion.45
  236.3 23.1 %reduce-scatter.16.cloned.1.call-done = bf16[1,256,768]{2,1,0:T(8,128)(2,1)} async-done(((bf16[1,1024,768]{2,1,0:T(8,128)(2,1)}), bf16[1,256,768]{2,1,0:T(8,128)(2,1)}) %reduce-scatter.16.cloned.1.call-update) | async-done | bytes 393232 | tf_op jit(solution)/shard_map/reduce_scatter | solution.py:202
  261.8 1.6 add_convert_fusion.1
  263.9 1.5 collective-permute-start
  265.5 2.9 fusion.108
  268.5 2.4 collective-permute-done
  272.7 1.5 collective-permute-start.1
  274.2 7.5 collective-permute-done.1
  283.7 2.4 collective-permute-start.2
  286.2 43.3 %all_gather.68 = bf16[64,12]{1,0:T(8,128)(2,1)S(1)} all-gather(bf16[8,12]{1,0:T(8,128)(2,1)} %param.31), channel_id=1, replica_groups=mesh['dp'=8,'tensor'=4] {'dp'}, dimensions={0}, use_global_device_ids=true | all-gather | bytes 1728 | tf_op jit(solution)/shard_map/all_gather | solution.py:179
  330.1 1.4 copy.63
  331.5 1.4 reshape.261
  332.9 1.4 pad_maximum_fusion
  334.3 1.2 reverse_select_fusion
  335.5 5.5 multiply_convert_fusion.1
  341.0 5.5 fusion.112
  347.7 2.6 fusion.47
  350.3 4.4 fusion.46
  354.8 1.3 convert_element_type.153
  356.0 21.2 %reduce-scatter.20.cloned.1.call-done = bf16[1,256,768]{2,1,0:T(8,128)(2,1)} async-done(((bf16[1,1024,768]{2,1,0:T(8,128)(2,1)}), bf16[1,256,768]{2,1,0:T(8,128)(2,1)}) %reduce-scatter.20.cloned.1.call-update) | async-done | bytes 393232 | tf_op jit(solution)/shard_map/reduce_scatter | solution.py:226
  377.2 2.0 fusion.89
  379.8 28.0 %reduce-scatter.18.cloned.1.call-done = bf16[1,256,768]{2,1,0:T(8,128)(2,1)} async-done(((bf16[1,1024,768]{2,1,0:T(8,128)(2,1)}), bf16[1,256,768]{2,1,0:T(8,128)(2,1)}) %reduce-scatter.18.cloned.1.call-update) | async-done | bytes 393232 | tf_op jit(solution)/shard_map/reduce_scatter | solution.py:212
  407.8 3.3 fusion.103
  412.9 19.6 %all-gather.16.cloned.1.call-done = bf16[1,1024,768]{2,1,0:T(8,128)(2,1)} async-done(((bf16[1,256,768]{2,1,0:T(8,128)(2,1)}), bf16[1,1024,768]{2,1,0:T(8,128)(2,1)}) %all-gather.16.cloned.1.call-update) | async-done | bytes 1572880 | tf_op jit(solution)/shard_map/all_gather | solution.py:235
  432.4 2.1 fusion.61
  434.6 7.5 fusion.106
  442.1 6.3 fusion.113
  448.4 19.8 %fusion.70 = bf16[3,64,1024]{2,1,0:T(8,128)(2,1)} fusion(bf16[1024,3,64]{0,2,1:T(8,128)(2,1)S(1)} %bitcast.149, f32[3,1024,1024]{1,2,0:T(8,128)} %fusion.113, f32[3,1024,1024]{1,2,0:T(8,128)} %copy-done, f32[3,1024]{1,0:T(4,128)S(1)} %log_add_fusion), kind=kOutput, calls=%fused_computation.62 | convolution fusion | flops 431165440 | bytes 25964544 | tf_op jit(solution)/shard_map/while/body/eval_jaxpr/hqk,qhd->khd/dot_general | solution.py:117
  468.2 20.0 %fusion.107 = (f32[3,64]{1,0:T(4,128)}, bf16[1024,3,64]{0,2,1:T(8,128)(2,1)}) fusion(bf16[1024,3,64]{0,2,1:T(8,128)(2,1)S(1)} %bitcast.147, f32[3,1024,1024]{1,2,0:T(8,128)} %fusion.113, f32[3,1024,1024]{1,2,0:T(8,128)} %copy-done, f32[3,1024]{1,0:T(4,128)S(1)} %log_add_fusion), kind=kOutput, calls=%fused_computation.126 | convolution fusion | flops 431361856 | bytes 25965312 | tf_op jit(solution)/shard_map/while/body/eval_jaxpr/hqk,khd->qhd/dot_general | solution.py:114
  488.3 1.7 fusion.115
  490.6 1.9 fusion.48
  492.6 4.7 fusion.29
  497.4 4.8 convolution_bitcast_fusion
  502.2 3.1 copy.81
  505.6 2.9 fusion.23
  508.6 1.6 fusion.33
  510.3 1.6 fusion.35
  513.4 1.5 fusion.37
  514.9 37.6 %all-reduce.16 = (f32[64,3]{0,1:T(4,128)S(1)}, f32[64,3]{0,1:T(4,128)S(1)}, f32[64,12]{0,1:T(8,128)S(1)}) all-reduce(f32[64,3]{0,1:T(4,128)} %bitcast.162, f32[64,3]{0,1:T(4,128)} %bitcast.161, f32[64,12]{0,1:T(8,128)S(1)} %bitcast.158), channel_id=9, replica_groups=mesh['dp'=8,'tensor'=4] {'dp'}, use_global_device_ids=true, to_apply=%region_21.22.clone | all-reduce | flops 1152 | bytes 9216
  554.5 1.4 fusion.90
  556.0 38.3 %all-reduce.15 = (f32[768]{0:T(1024)S(1)}, f32[768]{0:T(1024)S(1)}, f32[768]{0:T(1024)S(1)}, f32[768]{0:T(1024)S(1)}, f32[768]{0:T(1024)S(1)}, /*index=5*/f32[768]{0:T(1024)S(1)}) all-reduce(f32[768]{0:T(1024)S(1)} %get-tuple-element.132, f32[768]{0:T(1024)S(1)} %get-tuple-element.137, ...), channel_id=6, replica_groups=mesh['dp'=8,'tensor'=4] {'dp','tensor'}, use_global_device_ids=true, to_apply=%region_16.17.clone | all-reduce | flops 4608 | bytes 36864
  597.8 2.2 fusion.83
  600.0 67.2 %reduce-scatter.34.cloned.1.call-done = f32[96,768]{1,0:T(8,128)} async-done(((f32[768,768]{1,0:T(8,128)}), f32[96,768]{1,0:T(8,128)}) %reduce-scatter.34.cloned.1.call-update) | async-done | bytes 294928
  667.1 65.4 %reduce-scatter.30.cloned.1.call-done = f32[96,192]{1,0:T(8,128)} async-done(((f32[768,192]{1,0:T(8,128)}), f32[96,192]{1,0:T(8,128)}) %reduce-scatter.30.cloned.1.call-update) | async-done | bytes 73744 | tf_op jit(solution)/shard_map/reduce_scatter | solution.py:285
  732.5 65.7 %reduce-scatter.28.cloned.1.call-done = f32[96,192]{1,0:T(8,128)} async-done(((f32[768,192]{1,0:T(8,128)}), f32[96,192]{1,0:T(8,128)}) %reduce-scatter.28.cloned.1.call-update) | async-done | bytes 73744 | tf_op jit(solution)/shard_map/reduce_scatter | solution.py:283
  798.3 65.5 %reduce-scatter.26.cloned.1.call-done = f32[96,192]{1,0:T(8,128)} async-done(((f32[768,192]{1,0:T(8,128)}), f32[96,192]{1,0:T(8,128)}) %reduce-scatter.26.cloned.1.call-update) | async-done | bytes 73744 | tf_op jit(solution)/shard_map/reduce_scatter | solution.py:282
  863.8 65.7 %reduce-scatter.24.cloned.1.call-done = f32[96,192]{1,0:T(8,128)} async-done(((f32[768,192]{1,0:T(8,128)}), f32[96,192]{1,0:T(8,128)}) %reduce-scatter.24.cloned.1.call-update) | async-done | bytes 73744 | tf_op jit(solution)/shard_map/reduce_scatter | solution.py:280
  (158 shorter events, 28.5 us)
Async XLA Ops:
  8.0 50.8 %copy-start.31 = (bf16[8,3]{0,1:T(4,128)(2,1)S(1)}, bf16[8,3]{0,1:T(4,128)(2,1)}, u32[]{:S(2)}) copy-start(bf16[8,3]{0,1:T(4,128)(2,1)} %param.22) | copy-start | bytes 148
  8.0 67.6 %copy-start.32 = (bf16[8,3]{0,1:T(4,128)(2,1)S(1)}, bf16[8,3]{0,1:T(4,128)(2,1)}, u32[]{:S(2)}) copy-start(bf16[8,3]{0,1:T(4,128)(2,1)} %param.25) | copy-start | bytes 148
  8.0 85.7 %copy-start.22 = (bf16[96,192]{1,0:T(8,128)(2,1)S(1)}, bf16[96,192]{1,0:T(8,128)(2,1)}, u32[]{:S(2)}) copy-start(bf16[96,192]{1,0:T(8,128)(2,1)} %param.21) | copy-start | bytes 110596
  8.1 116.8 %copy-start.23 = (bf16[96,192]{1,0:T(8,128)(2,1)S(1)}, bf16[96,192]{1,0:T(8,128)(2,1)}, u32[]{:S(2)}) copy-start(bf16[96,192]{1,0:T(8,128)(2,1)} %param.23) | copy-start | bytes 110596
  8.1 147.8 %copy-start.24 = (bf16[96,192]{1,0:T(8,128)(2,1)S(1)}, bf16[96,192]{1,0:T(8,128)(2,1)}, u32[]{:S(2)}) copy-start(bf16[96,192]{1,0:T(8,128)(2,1)} %param.24) | copy-start | bytes 110596
  8.1 178.9 %copy-start.25 = (bf16[96,192]{1,0:T(8,128)(2,1)S(1)}, bf16[96,192]{1,0:T(8,128)(2,1)}, u32[]{:S(2)}) copy-start(bf16[96,192]{1,0:T(8,128)(2,1)} %param.26) | copy-start | bytes 110596
  8.1 209.9 %all-gather.8.cloned.1.call-start = ((), (), s32[]{:S(2)}) async-start(), calls=%async_computation.10 | async-start | bytes 1966080 | tf_op jit(solution)/shard_map/all_gather | solution.py:186
  9.4 49.4 %copy-start.26 = (f32[256]{0:T(256)}, f32[256]{0:T(256)S(1)}, u32[]{:S(2)}) copy-start(f32[256]{0:T(256)S(1)} %broadcast_multiply_fusion.5) | copy-start | bytes 3076
  10.8 48.0 %copy-start.29 = (f32[256]{0:T(256)}, f32[256]{0:T(256)S(1)}, u32[]{:S(2)}) copy-start(f32[256]{0:T(256)S(1)} %add_rsqrt_fusion.1) | copy-start | bytes 3076
  56.6 68.2 %copy-start.20 = (f32[768]{0:T(1024)}, f32[768]{0:T(1024)S(1)}, u32[]{:S(2)}) copy-start(f32[768]{0:T(1024)S(1)} %convert_element_type.132) | copy-start | bytes 9220
  58.8 200.6 %reduce-scatter.16.cloned.1.call-start = ((), (), s32[]{:S(2)}) async-start(), calls=%async_computation.11 | async-start | bytes 1966080 | tf_op jit(solution)/shard_map/reduce_scatter | solution.py:202
  124.8 99.5 %copy-start.12 = (bf16[768,192]{1,0:T(8,128)(2,1)}, bf16[768,192]{1,0:T(8,128)(2,1)S(1)}, u32[]{:S(2)}) copy-start(bf16[768,192]{1,0:T(8,128)(2,1)S(1)} %all_gather.59) | copy-start | bytes 884740
  155.9 68.4 %copy-start.10 = (bf16[768,192]{1,0:T(8,128)(2,1)}, bf16[768,192]{1,0:T(8,128)(2,1)S(1)}, u32[]{:S(2)}) copy-start(bf16[768,192]{1,0:T(8,128)(2,1)S(1)} %all_gather.61) | copy-start | bytes 884740
  187.0 39.4 %copy-start.7 = (bf16[768,192]{1,0:T(8,128)(2,1)}, bf16[768,192]{1,0:T(8,128)(2,1)S(1)}, u32[]{:S(2)}) copy-start(bf16[768,192]{1,0:T(8,128)(2,1)S(1)} %all_gather.57) | copy-start | bytes 884740
  217.9 13.4 %copy-start.9 = (bf16[768,192]{1,0:T(8,128)(2,1)}, bf16[768,192]{1,0:T(8,128)(2,1)S(1)}, u32[]{:S(2)}) copy-start(bf16[768,192]{1,0:T(8,128)(2,1)S(1)} %all_gather.62) | copy-start | bytes 884740
  220.2 4.1 copy-start.14
  222.4 1.9 copy-start.16
  224.3 4.7 copy-start
  224.3 2.6 copy-start.1
  231.3 0.7 copy-start.5
  231.3 28.1 %copy-start.2 = (f32[1,256,768]{2,1,0:T(8,128)S(1)}, f32[1,256,768]{2,1,0:T(8,128)}, u32[]{:S(2)}) copy-start(f32[1,256,768]{2,1,0:T(8,128)} %param.17) | copy-start | bytes 2359300
  233.9 101.6 %all-gather.12.cloned.1.call-start = ((), (), s32[]{:S(2)}) async-start(), calls=%async_computation.13 | async-start | bytes 1327104 | tf_op jit(solution)/shard_map/all_gather | solution.py:178
  234.5 101.0 %all-gather.10.cloned.1.call-start = ((), (), s32[]{:S(2)}) async-start(), calls=%async_computation.12 | async-start | bytes 1966080 | tf_op jit(solution)/shard_map/all_gather | solution.py:207
  260.6 0.6 copy-start.28
  261.2 0.6 copy-start.30
  263.4 77.6 %all-gather.14.cloned.1.call-start = ((), (), s32[]{:S(2)}) async-start(), calls=%async_computation.15 | async-start | bytes 1966080 | tf_op jit(solution)/shard_map/all_gather | solution.py:217
  263.9 6.9 collective-permute-start
  268.4 108.8 %reduce-scatter.20.cloned.1.call-start = ((), (), s32[]{:S(2)}) async-start(), calls=%async_computation.16 | async-start | bytes 1966080 | tf_op jit(solution)/shard_map/reduce_scatter | solution.py:226
  272.7 8.9 collective-permute-start.1
  283.7 49.2 %collective-permute-start.2 = (bf16[4,96,768]{2,1,0:T(8,128)(2,1)}, bf16[4,96,768]{2,1,0:T(8,128)(2,1)}, u32[]{:S(2)}, u32[]{:S(2)}) collective-permute-start(bf16[4,96,768]{2,1,0:T(8,128)(2,1)} %bitcast.21), channel_id=1, source_target_pairs={{0,16},{4,20},{8,24},{12,28},{16,0},{20,4},{24,8},{28,12},{1,17},{... | collective-permute-start | bytes 1769480 | tf_op jit(solution)/shard_map/ppermute | solution.py:24
  341.0 6.7 copy-start.33
  346.5 1.2 copy-start.34
  350.3 57.6 %reduce-scatter.18.cloned.1.call-start = ((), (), s32[]{:S(2)}) async-start(), calls=%async_computation.14 | async-start | bytes 1966080 | tf_op jit(solution)/shard_map/reduce_scatter | solution.py:212
  354.7 77.8 %all-gather.16.cloned.1.call-start = ((), (), s32[]{:S(2)}) async-start(), calls=%async_computation.17 | async-start | bytes 1966080 | tf_op jit(solution)/shard_map/all_gather | solution.py:235
  411.1 0.9 copy-start.3
  412.8 141.7 %reduce-scatter.22.cloned.1.call-start = ((), (), s32[]{:S(2)}) async-start(), calls=%async_computation.18 | async-start | bytes 1966080 | tf_op jit(solution)/shard_map/reduce_scatter | solution.py:260
  442.1 6.3 copy-start.17
  448.4 19.8 %copy-start.15 = (bf16[1024,192]{0,1:T(8,128)(2,1)S(1)}, bf16[1024,192]{0,1:T(8,128)(2,1)}, u32[]{:S(2)}) copy-start(bf16[1024,192]{0,1:T(8,128)(2,1)} %copy-done.14) | copy-start | bytes 1179652
  468.2 20.0 %copy-start.11 = (bf16[768,192]{1,0:T(8,128)(2,1)S(1)}, bf16[768,192]{1,0:T(8,128)(2,1)}, u32[]{:S(2)}) copy-start(bf16[768,192]{1,0:T(8,128)(2,1)} %copy-done.10) | copy-start | bytes 884740
  488.2 1.7 copy-start.13
  488.2 1.7 copy-start.18
  488.2 2.4 copy-start.8
  492.5 107.5 %reduce-scatter.32.cloned.1.call-start = ((), (), s32[]{:S(2)}) async-start(), calls=%async_computation.23 | async-start | bytes 2654208 | tf_op jit(solution)/shard_map/reduce_scatter | solution.py:286
  497.3 169.8 %reduce-scatter.34.cloned.1.call-start = ((), (), s32[]{:S(2)}) async-start(), calls=%async_computation.24 | async-start | bytes 2654208
  502.2 3.4 copy-start.6
  505.3 227.2 %reduce-scatter.30.cloned.1.call-start = ((), (), s32[]{:S(2)}) async-start(), calls=%async_computation.22 | async-start | bytes 884736 | tf_op jit(solution)/shard_map/reduce_scatter | solution.py:285
  508.5 1.7 copy-start.19
  508.6 289.7 %reduce-scatter.28.cloned.1.call-start = ((), (), s32[]{:S(2)}) async-start(), calls=%async_computation.21 | async-start | bytes 884736 | tf_op jit(solution)/shard_map/reduce_scatter | solution.py:283
  510.2 44.4 %copy-start.21 = (f32[768]{0:T(1024)S(1)}, f32[768]{0:T(1024)}, u32[]{:S(2)}) copy-start(f32[768]{0:T(1024)} %copy-done.20) | copy-start | bytes 9220
  510.2 44.3 %copy-start.27 = (f32[256]{0:T(256)S(1)}, f32[256]{0:T(256)}, u32[]{:S(2)}) copy-start(f32[256]{0:T(256)} %copy-done.26) | copy-start | bytes 3076
  510.2 353.6 %reduce-scatter.26.cloned.1.call-start = ((), (), s32[]{:S(2)}) async-start(), calls=%async_computation.20 | async-start | bytes 884736 | tf_op jit(solution)/shard_map/reduce_scatter | solution.py:282
  511.8 86.0 %copy-start.4 = (f32[1,256,768]{2,1,0:T(8,128)S(1)}, f32[1,256,768]{2,1,0:T(8,128)}, u32[]{:S(2)}) copy-start(f32[1,256,768]{2,1,0:T(8,128)} %copy-done.3) | copy-start | bytes 2359300
  511.9 417.6 %reduce-scatter.24.cloned.1.call-start = ((), (), s32[]{:S(2)}) async-start(), calls=%async_computation.19 | async-start | bytes 884736 | tf_op jit(solution)/shard_map/reduce_scatter | solution.py:280
Sparse Core Ops, SparseCore 0:
  58.9 16.9 all-gather.7
  234.0 25.3 reduce-scatter.15
  350.4 26.8 reduce-scatter.19
  379.6 28.1 reduce-scatter.17
Sparse Core Ops, SparseCore 1:
  236.8 38.4 all-gather.11
  277.4 18.4 all-gather.9
  297.4 19.5 all-gather.13
  412.9 19.5 all-gather.15
  492.6 28.1 reduce-scatter.21
  524.9 70.2 reduce-scatter.31
  599.0 68.1 reduce-scatter.33
  670.9 61.6 reduce-scatter.29
  736.6 61.6 reduce-scatter.27
  802.2 61.6 reduce-scatter.25
  867.9 61.5 reduce-scatter.23
